TPU v7x, 128 devices: a whole 4x4x4 slice. The times are simulated.
128 devices in a mesh: patch: 32 (over x, z, core), grp: 4 (over y).
Axes of the slice: x: 4, y: 4, z: 4, core: 2. Of those that a mesh axis runs over, the one named last changes fastest.
Arguments:
- incident: float32 [16, 262144], P(None, ('patch', 'grp')), may hold values from -6 to 6
- self_term: float32 [262144], P(('patch', 'grp')), may hold values from 1 to 3
- near_field: bfloat16 [262144, 2304], P(('patch', 'grp')), may hold values from -0.125 to 0.125
- history: bfloat16 [8, 16, 262144], P(None, None, 'patch'), may hold values from -6 to 6
- ret_values: bfloat16 [32768, 128, 128], P(('patch', 'grp')), may hold values from -0.125 to 0.125
- slot_row: int32 [32768], P(('patch', 'grp')), may hold values from 0 to 15
- slot_col: int32 [32768], P(('patch', 'grp')), may hold values from 0 to 191
- slot_delay: int32 [32768], P(('patch', 'grp')), may hold values from 0 to 7
- live_count: int32 [128], P(('patch', 'grp')), may hold values from 32 to 256, as said below
Outputs:
- current: float32 [16, 262144], P(None, ('patch', 'grp'))
- newest: bfloat16 [16, 262144], P(None, 'patch')
Inputs may be any that keep to these rules, and one draw needn't show every extreme that they name: The first live_count[d] slots of shard d are live, the rest ignored; some shard has all 256 slots live.
All inputs are finite; a program needn't handle non-finite values.
Results may differ from a plain program's by a relative error of at most 0.0055.
Values may be sent and summed in bfloat16 or wider, within the bound.
No kernel may reach another device: no remote copies, remote signals or barrier semaphores. Data moves between devices by JAX's collectives and lax.ppermute only.
A program may use at most 128 MiB of HBM per device.

v0:
```python
import jax
import jax.numpy as jnp
from jax import lax
from jax.sharding import PartitionSpec as P

BLK = 128
DELAYS = 8
SWEEPS = 4
RB = 16
SLOTS = 256


def extended_2(block, sides, width):
    for axis, dim in sides:
        count = lax.axis_size(axis)
        forward = [(i, i + 1) for i in range(count - 1)]
        backward = [(target, source) for source, target in forward]
        low = lax.ppermute(
            lax.slice_in_dim(block, block.shape[dim] - width, None, axis=dim), axis, forward
        )
        high = lax.ppermute(lax.slice_in_dim(block, 0, width, axis=dim), axis, backward)
        block = jnp.concatenate([low, block, high], axis=dim)
    return block


def body(
    incident, self_term, near_field, history, ret_values, slot_row, slot_col, slot_delay, live_count
):
    waves = incident.shape[0]
    own_cols = incident.shape[1]
    group_idx = lax.axis_index("grp")
    window = extended_2(history, (("patch", 2),), history.shape[2])
    grouped = window.reshape(DELAYS, waves, window.shape[2] // BLK, BLK)
    limit = live_count[0]
    blocks = grouped[slot_delay, :, slot_col, :]
    prods = jnp.einsum("swj,sij->swi", blocks, ret_values, preferred_element_type=jnp.float32)
    alive = (jnp.arange(SLOTS, dtype=jnp.int32) < limit).astype(jnp.float32)
    onehot = (slot_row[None, :] == jnp.arange(RB, dtype=jnp.int32)[:, None]).astype(
        jnp.float32
    ) * alive[None, :]
    retarded = jnp.einsum("rs,swi->wri", onehot, prods, precision=lax.Precision.HIGHEST)
    rhs = incident - retarded.reshape(waves, own_cols)
    sweep_in = lax.dynamic_slice_in_dim(history[0], group_idx * own_cols, own_cols, 1)
    current = sweep_in.astype(jnp.float32)
    for sweep in range(SWEEPS):
        extended = extended_2(sweep_in, (("patch", 1),), BLK)
        coupling = lax.dot_general(
            extended, near_field, (((1,), (1,)), ((), ())), preferred_element_type=jnp.float32
        )
        current = (rhs - coupling) / self_term[None, :]
        sweep_in = current.astype(jnp.bfloat16)
    newest = lax.all_gather(sweep_in, "grp", axis=1, tiled=True)
    return (current, newest)


def solution(mesh):
    placed = (
        P(None, ("patch", "grp")),
        P(("patch", "grp")),
        P(("patch", "grp"), None),
        P(None, None, "patch"),
        P(("patch", "grp"), None, None),
        P(("patch", "grp")),
        P(("patch", "grp")),
        P(("patch", "grp")),
        P(("patch", "grp")),
    )
    return jax.shard_map(
        body,
        mesh=mesh,
        in_specs=placed,
        out_specs=(P(None, ("patch", "grp")), P(None, "patch")),
        check_vma=False,
    )
```

profile of v0, /device:TPU:6, one launch (start us, length us, event | category | flops | bytes accessed | tf_op | source)
XLA Modules:
  0.0 111.1 jit_solution(12761360910164445370)
XLA Ops:
  0.6 5.7 %collective-permute-start.1 = (bf16[8,16,8192]{2,1,0:T(8,128)(2,1)}, bf16[8,16,8192]{2,1,0:T(8,128)(2,1)S(1)}, u32[]{:S(2)}, u32[]{:S(2)}) collective-permute-start(bf16[8,16,8192]{2,1,0:T(8,128)(2,1)} %param.12), channel_id=1, source_target_pairs={{4,0},{8,4},{12,8},{16,12},{20,16},{24,20},{28,24},{32,28},{36,32}... | collective-permute-start | bytes 6291464 | tf_op jit(solution)/shard_map/ppermute | solution.py:21
  6.3 1.9 %collective-permute-start = (bf16[8,16,8192]{2,1,0:T(8,128)(2,1)}, bf16[8,16,8192]{2,1,0:T(8,128)(2,1)}, u32[]{:S(2)}, u32[]{:S(2)}) collective-permute-start(bf16[8,16,8192]{2,1,0:T(8,128)(2,1)} %param.12), channel_id=1, source_target_pairs={{0,4},{4,8},{8,12},{12,16},{16,20},{20,24},{24,28},{28,32},{32,36}... | collective-permute-start | bytes 6291464 | tf_op jit(solution)/shard_map/ppermute | solution.py:18
  8.2 1.0 slice.27
  9.2 5.8 %collective-permute-start.3 = (bf16[16,128]{1,0:T(8,128)(2,1)S(1)}, bf16[16,128]{1,0:T(8,128)(2,1)S(1)}, u32[]{:S(2)}, u32[]{:S(2)}) collective-permute-start(bf16[16,128]{1,0:T(8,128)(2,1)S(1)} %get-tuple-element.9), channel_id=1, source_target_pairs={{4,0},{8,4},{12,8},{16,12},{20,16},{24,20},{28,24},{32,28},{36,32}... | collective-permute-start | bytes 12296 | tf_op jit(solution)/shard_map/ppermute | solution.py:21
  15.0 1.9 %collective-permute-start.2 = (bf16[16,128]{1,0:T(8,128)(2,1)S(1)}, bf16[16,128]{1,0:T(8,128)(2,1)S(1)}, u32[]{:S(2)}, u32[]{:S(2)}) collective-permute-start(bf16[16,128]{1,0:T(8,128)(2,1)S(1)} %get-tuple-element.8), channel_id=1, source_target_pairs={{0,4},{4,8},{8,12},{12,16},{16,20},{20,24},{24,28},{28,32},{32,36}... | collective-permute-start | bytes 12296 | tf_op jit(solution)/shard_map/ppermute | solution.py:18
  17.6 0.7 fusion.36
  18.3 11.8 %collective-permute-done.1 = bf16[8,16,8192]{2,1,0:T(8,128)(2,1)S(1)} collective-permute-done((bf16[8,16,8192]{2,1,0:T(8,128)(2,1)}, bf16[8,16,8192]{2,1,0:T(8,128)(2,1)S(1)}, u32[]{:S(2)}, u32[]{:S(2)}) %collective-permute-start.1) | collective-permute-done | bytes 2097184 | tf_op jit(solution)/shard_map/ppermute | solution.py:21
  30.1 5.9 %collective-permute-done = bf16[8,16,8192]{2,1,0:T(8,128)(2,1)} collective-permute-done((bf16[8,16,8192]{2,1,0:T(8,128)(2,1)}, bf16[8,16,8192]{2,1,0:T(8,128)(2,1)}, u32[]{:S(2)}, u32[]{:S(2)}) %collective-permute-start) | collective-permute-done | bytes 2097184 | tf_op jit(solution)/shard_map/ppermute | solution.py:18
  36.1 7.2 %copy_bitcast_fusion = bf16[8,16,192,128]{3,1,2,0:T(8,128)(2,1)} fusion(bf16[8,16,8192]{2,1,0:T(8,128)(2,1)S(1)} %collective-permute-done.1, bf16[8,16,8192]{2,1,0:T(8,128)(2,1)} %param.12, bf16[8,16,8192]{2,1,0:T(8,128)(2,1)} %collective-permute-done), kind=kLoop, calls=%fused_computation.1 | loop fusion | flops 18874368 | bytes 12582912 | tf_op jit(solution)/shard_map/reshape | solution.py:33
  43.2 4.0 %gather_fusion = bf16[256,16,128]{2,1,0:T(8,128)(2,1)S(1)} fusion(bf16[8,16,192,128]{3,1,2,0:T(8,128)(2,1)} %copy_bitcast_fusion, s32[256]{0:T(256)S(1)} %fusion.36), kind=kCustom, calls=%fused_computation | custom fusion | bytes 2099200 | tf_op jit(solution)/shard_map/gather | solution.py:35
  47.2 0.0 copy-start.2
  47.3 0.0 copy-start.1
  47.3 0.0 copy-start
  47.3 0.0 slice-start
  47.3 0.0 slice-start.1
  47.3 6.9 %fusion.49 = f32[256,16,128]{2,1,0:T(8,128)S(1)} fusion(bf16[256,16,128]{2,1,0:T(8,128)(2,1)S(1)} %gather_fusion, bf16[256,128,128]{2,1,0:T(8,128)(2,1)} %param.13), kind=kOutput, calls=%fused_computation.62 | convolution fusion | flops 134217728 | bytes 11534336 | tf_op jit(solution)/shard_map/swj,sij->swi/dot_general | solution.py:36
  54.2 0.0 copy-done.2
  54.2 1.8 %fusion.7 = f32[16,128,16]{1,2,0:T(8,128)S(1)} fusion(f32[256,16,128]{2,1,0:T(8,128)S(1)} %fusion.49, f32[256]{0:T(256)S(1)} %compare_convert_fusion, s32[256]{0:T(256)S(1)} %copy-done.2), kind=kOutput, calls=%fused_computation.14 | convolution fusion | flops 100671488 | bytes 2230272 | tf_op jit(solution)/shard_map/rs,swi->wri/dot_general | solution.py:41
  56.0 0.0 copy-done.1
  56.0 0.1 bitcast_subtract_fusion
  56.0 0.0 slice-start.2
  56.1 0.0 collective-permute-done.3
  56.1 0.0 collective-permute-done.2
  56.1 0.0 copy-done
  56.1 6.3 %fusion.4 = bf16[16,2048]{1,0:T(8,128)(2,1)S(1)} fusion(f32[16,2048]{1,0:T(8,128)S(1)} %bitcast_subtract_fusion, bf16[2048,2304]{1,0:T(8,128)(2,1)} %param.11, bf16[16,128]{1,0:T(8,128)(2,1)S(1)} %collective-permute-done.3, bf16[16,2048]{1,0:T(8,128)(2,1)S(1)} %dynamic-slice_bitcast_fusion, bf16[16,128]{1,0:T(8,128)(2,1)S(1)} %collective-permute-done.2, ...), kind=kOutput, calls=%fused_computation.11 | convolution fusion | flops 151314432 | bytes 9715712 | tf_op jit(solution)/shard_map/dot_general | solution.py:47
  62.4 1.9 %collective-permute-start.5 = (bf16[16,128]{1,0:T(8,128)(2,1)S(1)}, bf16[16,128]{1,0:T(8,128)(2,1)S(1)}, u32[]{:S(2)}, u32[]{:S(2)}) collective-permute-start(bf16[16,128]{1,0:T(8,128)(2,1)S(1)} %get-tuple-element.7), channel_id=1, source_target_pairs={{4,0},{8,4},{12,8},{16,12},{20,16},{24,20},{28,24},{32,28},{36,32}... | collective-permute-start | bytes 12296 | tf_op jit(solution)/shard_map/ppermute | solution.py:21
  64.3 2.4 %collective-permute-start.4 = (bf16[16,128]{1,0:T(8,128)(2,1)S(1)}, bf16[16,128]{1,0:T(8,128)(2,1)S(1)}, u32[]{:S(2)}, u32[]{:S(2)}) collective-permute-start(bf16[16,128]{1,0:T(8,128)(2,1)S(1)} %get-tuple-element.6), channel_id=1, source_target_pairs={{0,4},{4,8},{8,12},{12,16},{16,20},{20,24},{24,28},{28,32},{32,36}... | collective-permute-start | bytes 12296 | tf_op jit(solution)/shard_map/ppermute | solution.py:18
  66.8 0.0 collective-permute-done.5
  66.8 4.6 %collective-permute-done.4 = bf16[16,128]{1,0:T(8,128)(2,1)S(1)} collective-permute-done((bf16[16,128]{1,0:T(8,128)(2,1)S(1)}, bf16[16,128]{1,0:T(8,128)(2,1)S(1)}, u32[]{:S(2)}, u32[]{:S(2)}) %collective-permute-start.4) | collective-permute-done | bytes 4128 | tf_op jit(solution)/shard_map/ppermute | solution.py:18
  71.4 0.0 slice-done
  71.4 0.0 slice-done.1
  71.4 0.0 slice-done.2
  71.4 2.5 %fusion.5 = bf16[16,2048]{1,0:T(8,128)(2,1)S(1)} fusion(f32[16,2048]{1,0:T(8,128)S(1)} %bitcast_subtract_fusion, bf16[2048,2304]{1,0:T(8,128)(2,1)S(1)} %bitcast.23, bf16[16,128]{1,0:T(8,128)(2,1)S(1)} %collective-permute-done.5, bf16[16,2048]{1,0:T(8,128)(2,1)S(1)} %fusion.4, bf16[16,128]{1,0:T(8,128)(2,1)S(1)} %collective-permute-done.4, f32[2048]{0:T(1024)S(1)} %copy-done), kind=kOutput, calls=%fused_computation.12 | convolution fusion | flops 151314432 | bytes 9715712 | tf_op jit(solution)/shard_map/dot_general | solution.py:47
  73.9 1.9 %collective-permute-start.7 = (bf16[16,128]{1,0:T(8,128)(2,1)S(1)}, bf16[16,128]{1,0:T(8,128)(2,1)S(1)}, u32[]{:S(2)}, u32[]{:S(2)}) collective-permute-start(bf16[16,128]{1,0:T(8,128)(2,1)S(1)} %get-tuple-element.5), channel_id=1, source_target_pairs={{4,0},{8,4},{12,8},{16,12},{20,16},{24,20},{28,24},{32,28},{36,32}... | collective-permute-start | bytes 12296 | tf_op jit(solution)/shard_map/ppermute | solution.py:21
  75.9 2.4 %collective-permute-start.6 = (bf16[16,128]{1,0:T(8,128)(2,1)S(1)}, bf16[16,128]{1,0:T(8,128)(2,1)S(1)}, u32[]{:S(2)}, u32[]{:S(2)}) collective-permute-start(bf16[16,128]{1,0:T(8,128)(2,1)S(1)} %get-tuple-element.4), channel_id=1, source_target_pairs={{0,4},{4,8},{8,12},{12,16},{16,20},{20,24},{24,28},{28,32},{32,36}... | collective-permute-start | bytes 12296 | tf_op jit(solution)/shard_map/ppermute | solution.py:18
  78.3 0.0 collective-permute-done.7
  78.3 4.6 %collective-permute-done.6 = bf16[16,128]{1,0:T(8,128)(2,1)S(1)} collective-permute-done((bf16[16,128]{1,0:T(8,128)(2,1)S(1)}, bf16[16,128]{1,0:T(8,128)(2,1)S(1)}, u32[]{:S(2)}, u32[]{:S(2)}) %collective-permute-start.6) | collective-permute-done | bytes 4128 | tf_op jit(solution)/shard_map/ppermute | solution.py:18
  82.9 2.5 %fusion.6 = bf16[16,2048]{1,0:T(8,128)(2,1)S(1)} fusion(f32[16,2048]{1,0:T(8,128)S(1)} %bitcast_subtract_fusion, bf16[2048,2304]{1,0:T(8,128)(2,1)S(1)} %bitcast.23, bf16[16,128]{1,0:T(8,128)(2,1)S(1)} %collective-permute-done.7, bf16[16,2048]{1,0:T(8,128)(2,1)S(1)} %fusion.5, bf16[16,128]{1,0:T(8,128)(2,1)S(1)} %collective-permute-done.6, f32[2048]{0:T(1024)S(1)} %copy-done), kind=kOutput, calls=%fused_computation.13 | convolution fusion | flops 151314432 | bytes 9715712 | tf_op jit(solution)/shard_map/dot_general | solution.py:47
  85.5 1.9 %collective-permute-start.9 = (bf16[16,128]{1,0:T(8,128)(2,1)S(1)}, bf16[16,128]{1,0:T(8,128)(2,1)S(1)}, u32[]{:S(2)}, u32[]{:S(2)}) collective-permute-start(bf16[16,128]{1,0:T(8,128)(2,1)S(1)} %get-tuple-element.3), channel_id=1, source_target_pairs={{4,0},{8,4},{12,8},{16,12},{20,16},{24,20},{28,24},{32,28},{36,32}... | collective-permute-start | bytes 12296 | tf_op jit(solution)/shard_map/ppermute | solution.py:21
  87.4 2.4 %collective-permute-start.8 = (bf16[16,128]{1,0:T(8,128)(2,1)S(1)}, bf16[16,128]{1,0:T(8,128)(2,1)S(1)}, u32[]{:S(2)}, u32[]{:S(2)}) collective-permute-start(bf16[16,128]{1,0:T(8,128)(2,1)S(1)} %get-tuple-element.2), channel_id=1, source_target_pairs={{0,4},{4,8},{8,12},{12,16},{16,20},{20,24},{24,28},{28,32},{32,36}... | collective-permute-start | bytes 12296 | tf_op jit(solution)/shard_map/ppermute | solution.py:18
  89.8 0.0 collective-permute-done.9
  89.8 4.6 %collective-permute-done.8 = bf16[16,128]{1,0:T(8,128)(2,1)S(1)} collective-permute-done((bf16[16,128]{1,0:T(8,128)(2,1)S(1)}, bf16[16,128]{1,0:T(8,128)(2,1)S(1)}, u32[]{:S(2)}, u32[]{:S(2)}) %collective-permute-start.8) | collective-permute-done | bytes 4128 | tf_op jit(solution)/shard_map/ppermute | solution.py:18
  94.4 3.2 %fusion.48 = (bf16[16,2048]{1,0:T(8,128)(2,1)S(1)}, f32[16,2048]{1,0:T(8,128)}) fusion(f32[2048]{0:T(1024)S(1)} %copy-done, f32[16,2048]{1,0:T(8,128)S(1)} %bitcast_subtract_fusion, bf16[2048,2304]{1,0:T(8,128)(2,1)S(1)} %bitcast.23, bf16[16,128]{1,0:T(8,128)(2,1)S(1)} %collective-permute-done.9, bf16[16,2048]{1,0:T(8,128)(2,1)S(1)} %fusion.6, ...), kind=kOutput, calls=%fused_computation.61 | convolution fusion | flops 151314432 | bytes 9846784 | tf_op jit(solution)/shard_map/dot_general | solution.py:47
  97.6 12.8 %all_gather.3 = bf16[16,8192]{1,0:T(8,128)(2,1)S(1)} all-gather(bf16[16,2048]{1,0:T(8,128)(2,1)S(1)} %get-tuple-element.10), channel_id=1, replica_groups=mesh['patch'=32,'grp'=4] {'grp'}, dimensions={1}, use_global_device_ids=true | all-gather | bytes 327680 | tf_op jit(solution)/shard_map/all_gather | solution.py:52
  110.4 0.7 copy.21
  (7 shorter events, 0.1 us)
Async XLA Ops:
  0.6 29.5 %collective-permute-start.1 = (bf16[8,16,8192]{2,1,0:T(8,128)(2,1)}, bf16[8,16,8192]{2,1,0:T(8,128)(2,1)S(1)}, u32[]{:S(2)}, u32[]{:S(2)}) collective-permute-start(bf16[8,16,8192]{2,1,0:T(8,128)(2,1)} %param.12), channel_id=1, source_target_pairs={{4,0},{8,4},{12,8},{16,12},{20,16},{24,20},{28,24},{32,28},{36,32}... | collective-permute-start | bytes 6291464 | tf_op jit(solution)/shard_map/ppermute | solution.py:21
  6.3 29.8 %collective-permute-start = (bf16[8,16,8192]{2,1,0:T(8,128)(2,1)}, bf16[8,16,8192]{2,1,0:T(8,128)(2,1)}, u32[]{:S(2)}, u32[]{:S(2)}) collective-permute-start(bf16[8,16,8192]{2,1,0:T(8,128)(2,1)} %param.12), channel_id=1, source_target_pairs={{0,4},{4,8},{8,12},{12,16},{16,20},{20,24},{24,28},{28,32},{32,36}... | collective-permute-start | bytes 6291464 | tf_op jit(solution)/shard_map/ppermute | solution.py:18
  9.2 46.8 %collective-permute-start.3 = (bf16[16,128]{1,0:T(8,128)(2,1)S(1)}, bf16[16,128]{1,0:T(8,128)(2,1)S(1)}, u32[]{:S(2)}, u32[]{:S(2)}) collective-permute-start(bf16[16,128]{1,0:T(8,128)(2,1)S(1)} %get-tuple-element.9), channel_id=1, source_target_pairs={{4,0},{8,4},{12,8},{16,12},{20,16},{24,20},{28,24},{32,28},{36,32}... | collective-permute-start | bytes 12296 | tf_op jit(solution)/shard_map/ppermute | solution.py:21
  15.0 41.1 %collective-permute-start.2 = (bf16[16,128]{1,0:T(8,128)(2,1)S(1)}, bf16[16,128]{1,0:T(8,128)(2,1)S(1)}, u32[]{:S(2)}, u32[]{:S(2)}) collective-permute-start(bf16[16,128]{1,0:T(8,128)(2,1)S(1)} %get-tuple-element.8), channel_id=1, source_target_pairs={{0,4},{4,8},{8,12},{12,16},{16,20},{20,24},{24,28},{28,32},{32,36}... | collective-permute-start | bytes 12296 | tf_op jit(solution)/shard_map/ppermute | solution.py:18
  47.2 7.0 %copy-start.2 = (s32[256]{0:T(256)S(1)}, s32[256]{0:T(256)}, u32[]{:S(2)}) copy-start(s32[256]{0:T(256)} %param.14) | copy-start | bytes 3076
  47.3 8.7 %copy-start.1 = (f32[16,2048]{1,0:T(8,128)S(1)}, f32[16,2048]{1,0:T(8,128)}, u32[]{:S(2)}) copy-start(f32[16,2048]{1,0:T(8,128)} %param.9) | copy-start | bytes 393220
  47.3 8.8 %copy-start = (f32[2048]{0:T(1024)S(1)}, f32[2048]{0:T(1024)}, u32[]{:S(2)}) copy-start(f32[2048]{0:T(1024)} %param.10) | copy-start | bytes 24580
  47.3 24.1 %slice-start = ((s8[9437184]{0:T(1024)(128)(4,1)}), s8[4194304]{0:T(1024)(128)(4,1)S(1)}, s32[]{:S(2)}) async-start(s8[9437184]{0:T(1024)(128)(4,1)} %bitcast.22), calls=%async_computation | async-start | bytes 8388608
  47.3 24.1 %slice-start.1 = ((s8[9437184]{0:T(1024)(128)(4,1)}), s8[4194304]{0:T(1024)(128)(4,1)S(1)}, s32[]{:S(2)}) async-start(s8[9437184]{0:T(1024)(128)(4,1)} %bitcast.22), calls=%async_computation.1 | async-start | bytes 8388608
  56.0 15.3 %slice-start.2 = ((s8[9437184]{0:T(1024)(128)(4,1)}), s8[1048576]{0:T(1024)(128)(4,1)S(1)}, s32[]{:S(2)}) async-start(s8[9437184]{0:T(1024)(128)(4,1)} %bitcast.22), calls=%async_computation.2 | async-start | bytes 2097152
  62.4 4.3 %collective-permute-start.5 = (bf16[16,128]{1,0:T(8,128)(2,1)S(1)}, bf16[16,128]{1,0:T(8,128)(2,1)S(1)}, u32[]{:S(2)}, u32[]{:S(2)}) collective-permute-start(bf16[16,128]{1,0:T(8,128)(2,1)S(1)} %get-tuple-element.7), channel_id=1, source_target_pairs={{4,0},{8,4},{12,8},{16,12},{20,16},{24,20},{28,24},{32,28},{36,32}... | collective-permute-start | bytes 12296 | tf_op jit(solution)/shard_map/ppermute | solution.py:21
  64.3 7.0 %collective-permute-start.4 = (bf16[16,128]{1,0:T(8,128)(2,1)S(1)}, bf16[16,128]{1,0:T(8,128)(2,1)S(1)}, u32[]{:S(2)}, u32[]{:S(2)}) collective-permute-start(bf16[16,128]{1,0:T(8,128)(2,1)S(1)} %get-tuple-element.6), channel_id=1, source_target_pairs={{0,4},{4,8},{8,12},{12,16},{16,20},{20,24},{24,28},{28,32},{32,36}... | collective-permute-start | bytes 12296 | tf_op jit(solution)/shard_map/ppermute | solution.py:18
  73.9 4.3 %collective-permute-start.7 = (bf16[16,128]{1,0:T(8,128)(2,1)S(1)}, bf16[16,128]{1,0:T(8,128)(2,1)S(1)}, u32[]{:S(2)}, u32[]{:S(2)}) collective-permute-start(bf16[16,128]{1,0:T(8,128)(2,1)S(1)} %get-tuple-element.5), channel_id=1, source_target_pairs={{4,0},{8,4},{12,8},{16,12},{20,16},{24,20},{28,24},{32,28},{36,32}... | collective-permute-start | bytes 12296 | tf_op jit(solution)/shard_map/ppermute | solution.py:21
  75.9 7.0 %collective-permute-start.6 = (bf16[16,128]{1,0:T(8,128)(2,1)S(1)}, bf16[16,128]{1,0:T(8,128)(2,1)S(1)}, u32[]{:S(2)}, u32[]{:S(2)}) collective-permute-start(bf16[16,128]{1,0:T(8,128)(2,1)S(1)} %get-tuple-element.4), channel_id=1, source_target_pairs={{0,4},{4,8},{8,12},{12,16},{16,20},{20,24},{24,28},{28,32},{32,36}... | collective-permute-start | bytes 12296 | tf_op jit(solution)/shard_map/ppermute | solution.py:18
  85.5 4.3 %collective-permute-start.9 = (bf16[16,128]{1,0:T(8,128)(2,1)S(1)}, bf16[16,128]{1,0:T(8,128)(2,1)S(1)}, u32[]{:S(2)}, u32[]{:S(2)}) collective-permute-start(bf16[16,128]{1,0:T(8,128)(2,1)S(1)} %get-tuple-element.3), channel_id=1, source_target_pairs={{4,0},{8,4},{12,8},{16,12},{20,16},{24,20},{28,24},{32,28},{36,32}... | collective-permute-start | bytes 12296 | tf_op jit(solution)/shard_map/ppermute | solution.py:21
  87.4 7.0 %collective-permute-start.8 = (bf16[16,128]{1,0:T(8,128)(2,1)S(1)}, bf16[16,128]{1,0:T(8,128)(2,1)S(1)}, u32[]{:S(2)}, u32[]{:S(2)}) collective-permute-start(bf16[16,128]{1,0:T(8,128)(2,1)S(1)} %get-tuple-element.2), channel_id=1, source_target_pairs={{0,4},{4,8},{8,12},{12,16},{16,20},{20,24},{24,28},{28,32},{32,36}... | collective-permute-start | bytes 12296 | tf_op jit(solution)/shard_map/ppermute | solution.py:18
where the time goes:
time: 112 us; the launch traced here: 111 us
  waiting for transfers between devices  31.6 us (28%)
  starting transfers between devices  28.2 us (25%)
  matrix products  23.2 us (21%)
  blocking collectives  12.8 us (11%)
  other arithmetic  7.93 us (7%)
  local copies, waits for them, and re-layouts  5.77 us (5%)
  between operations  1.54 us (1%)
    ppermute x5, waiting for transfers between devices, extended_2(): lax.ppermute(lax.slice_in_dim(block, block.shape[dim] - width, None, axis...  19.8 us
    ppermute x5, starting transfers between devices, extended_2(): lax.ppermute(lax.slice_in_dim(block, 0, width, axis=dim), axis, backward)  17.2 us
    dot_general x4, matrix products, body(): lax.dot_general(extended, near_field, (((1,), (1,)), ((), ())), preferred...  14.6 us
    all_gather x1, blocking collectives, body(): newest = lax.all_gather(sweep_in, 'grp', axis=1, tiled=True)  12.8 us
    ppermute x5, waiting for transfers between devices, extended_2(): lax.ppermute(lax.slice_in_dim(block, 0, width, axis=dim), axis, backward)  11.9 us
    ppermute x5, starting transfers between devices, extended_2(): lax.ppermute(lax.slice_in_dim(block, block.shape[dim] - width, None, axis...  11.1 us
    reshape x1, other arithmetic, body(): grouped = window.reshape(DELAYS, waves, window.shape[2] // BLK, BLK)  7.16 us
    dot_general x1, matrix products, body(): jnp.einsum('swj,sij->swi', blocks, ret_values, preferred_element_type=jnp...  6.91 us
  transfers between devices with their start and end apart: 10, of which 5 were waited for; matrix products, arithmetic and copies ran while one was open for 19% of the time, Pallas kernels for 0%

commit v1 on v0

--- a/solution.py
+++ b/solution.py
@@ -8,6 +8,34 @@
 SWEEPS = 4
 RB = 16
 SLOTS = 256
+
+
+def order_the_forms(values):
+    v1, extra, latest = (lax.axis_size("grp"), lax.axis_index("grp"), values.shape[1])
+    items = []
+    for num, dev_j in enumerate(values.shape):
+        items.append(dev_j * v1 if num == 1 else dev_j)
+    local_part = lax.dynamic_update_slice_in_dim(
+        jnp.zeros(items, values.dtype), values, extra * latest, axis=1
+    )
+    r2 = tall = values
+    for rr in range(1, v1 // 2 + 1):
+        so_far_all = []
+        for num in range(v1):
+            so_far_all.append((num, (num + 1) % v1))
+        r2 = lax.ppermute(r2, axis_name="grp", perm=so_far_all)
+        local_part = lax.dynamic_update_slice_in_dim(
+            local_part, r2, (extra - rr) % v1 * latest, axis=1
+        )
+        if 2 * rr < v1:
+            table = []
+            for num in range(v1):
+                table.append((num, (num - 1) % v1))
+            tall = lax.ppermute(tall, axis_name="grp", perm=table)
+            local_part = lax.dynamic_update_slice_in_dim(
+                local_part, tall, (extra + rr) % v1 * latest, axis=1
+            )
+    return local_part
 
 
 def extended_2(block, sides, width):
@@ -49,7 +77,7 @@
         )
         current = (rhs - coupling) / self_term[None, :]
         sweep_in = current.astype(jnp.bfloat16)
-    newest = lax.all_gather(sweep_in, "grp", axis=1, tiled=True)
+    newest = order_the_forms(sweep_in)
     return (current, newest)
 
 

time: 112 us -> 105 us (0.938)
  starting transfers between devices: 28.2 us -> 41.9 us
  blocking collectives: 12.8 us -> 0 us
  waiting for transfers between devices: 31.6 us -> 25.5 us
  other arithmetic: 7.93 us -> 6.43 us
    all_gather x1 -> x0, blocking collectives: 12.8 us -> none  [body(): newest = lax.all_gather(sweep_in, 'grp', axis=1, tiled=True)]
    ppermute x5, starting transfers between devices: 17.2 us -> 28.9 us  [extended_2(): lax.ppermute(lax.slice_in_dim(block, 0, width, axis=dim), axis, backward)]
    ppermute x0 -> x3, waiting for transfers between devices: none -> 7.87 us  [the longest x2 7.87 us: order_the_forms(): r2 = lax.ppermute(r2, axis_name='grp', perm=so_far_all)]
    ppermute x5, waiting for transfers between devices: 19.8 us -> 11.9 us  [extended_2(): lax.ppermute(lax.slice_in_dim(block, block.shape[dim] - width, None, axis...]
    ppermute x5, waiting for transfers between devices: 11.9 us -> 5.75 us  [extended_2(): lax.ppermute(lax.slice_in_dim(block, 0, width, axis=dim), axis, backward)]
    ppermute x0 -> x3, starting transfers between devices: none -> 3.32 us  [the longest x2 1.66 us: order_the_forms(): r2 = lax.ppermute(r2, axis_name='grp', perm=so_far_all)]
    reshape x1, other arithmetic: 7.16 us -> 5.67 us  [body(): grouped = window.reshape(DELAYS, waves, window.shape[2] // BLK, BLK)]
    ppermute x5, starting transfers between devices: 11.1 us -> 9.68 us  [extended_2(): lax.ppermute(lax.slice_in_dim(block, block.shape[dim] - width, None, axis...]
  transfers between devices with their start and end apart: 10 -> 13, of which waited for: 5 -> 7; matrix products, arithmetic and copies ran while one was open for 19% -> 19% of each run, Pallas kernels for 0% -> 0%
where the time goes in v1:
time: 105 us; the launch traced here: 104 us
  starting transfers between devices  41.9 us (40%)
  waiting for transfers between devices  25.5 us (24%)
  matrix products  23.2 us (22%)
  other arithmetic  6.43 us (6%)
  local copies, waits for them, and re-layouts  5.82 us (6%)
  between operations  1.57 us (1%)
    ppermute x5, starting transfers between devices, extended_2(): lax.ppermute(lax.slice_in_dim(block, 0, width, axis=dim), axis, backward)  28.9 us
    dot_general x4, matrix products, body(): lax.dot_general(extended, near_field, (((1,), (1,)), ((), ())), preferred...  14.6 us
    ppermute x5, waiting for transfers between devices, extended_2(): lax.ppermute(lax.slice_in_dim(block, block.shape[dim] - width, None, axis...  11.9 us
    ppermute x5, starting transfers between devices, extended_2(): lax.ppermute(lax.slice_in_dim(block, block.shape[dim] - width, None, axis...  9.68 us
    ppermute x2, waiting for transfers between devices, order_the_forms(): r2 = lax.ppermute(r2, axis_name='grp', perm=so_far_all)  7.87 us
    dot_general x1, matrix products, body(): jnp.einsum('swj,sij->swi', blocks, ret_values, preferred_element_type=jnp...  6.91 us
    ppermute x5, waiting for transfers between devices, extended_2(): lax.ppermute(lax.slice_in_dim(block, 0, width, axis=dim), axis, backward)  5.75 us
    reshape x1, other arithmetic, body(): grouped = window.reshape(DELAYS, waves, window.shape[2] // BLK, BLK)  5.67 us
  transfers between devices with their start and end apart: 13, of which 7 were waited for; matrix products, arithmetic and copies ran while one was open for 19% of the time, Pallas kernels for 0%

profile of v1, /device:TPU:6, one launch (start us, length us, event | category | flops | bytes accessed | tf_op | source)
XLA Modules:
  0.0 104.5 jit_solution(6769765879820422670)
XLA Ops:
  0.6 1.9 %collective-permute-start = (bf16[8,16,8192]{2,1,0:T(8,128)(2,1)}, bf16[8,16,8192]{2,1,0:T(8,128)(2,1)S(1)}, u32[]{:S(2)}, u32[]{:S(2)}) collective-permute-start(bf16[8,16,8192]{2,1,0:T(8,128)(2,1)} %param.12), channel_id=1, source_target_pairs={{0,4},{4,8},{8,12},{12,16},{16,20},{20,24},{24,28},{28,32},{32,36}... | collective-permute-start | bytes 6291464 | tf_op jit(solution)/shard_map/ppermute | solution.py:46
  2.6 5.8 %collective-permute-start.1 = (bf16[8,16,8192]{2,1,0:T(8,128)(2,1)}, bf16[8,16,8192]{2,1,0:T(8,128)(2,1)}, u32[]{:S(2)}, u32[]{:S(2)}) collective-permute-start(bf16[8,16,8192]{2,1,0:T(8,128)(2,1)} %param.12), channel_id=1, source_target_pairs={{4,0},{8,4},{12,8},{16,12},{20,16},{24,20},{28,24},{32,28},{36,32}... | collective-permute-start | bytes 6291464 | tf_op jit(solution)/shard_map/ppermute | solution.py:49
  8.3 1.0 slice.27
  9.3 1.9 %collective-permute-start.2 = (bf16[16,128]{1,0:T(8,128)(2,1)S(1)}, bf16[16,128]{1,0:T(8,128)(2,1)S(1)}, u32[]{:S(2)}, u32[]{:S(2)}) collective-permute-start(bf16[16,128]{1,0:T(8,128)(2,1)S(1)} %get-tuple-element.10), channel_id=1, source_target_pairs={{0,4},{4,8},{8,12},{12,16},{16,20},{20,24},{24,28},{28,32},{32,36}... | collective-permute-start | bytes 12296 | tf_op jit(solution)/shard_map/ppermute | solution.py:46
  11.3 5.8 %collective-permute-start.3 = (bf16[16,128]{1,0:T(8,128)(2,1)S(1)}, bf16[16,128]{1,0:T(8,128)(2,1)S(1)}, u32[]{:S(2)}, u32[]{:S(2)}) collective-permute-start(bf16[16,128]{1,0:T(8,128)(2,1)S(1)} %get-tuple-element.11), channel_id=1, source_target_pairs={{4,0},{8,4},{12,8},{16,12},{20,16},{24,20},{28,24},{32,28},{36,32}... | collective-permute-start | bytes 12296 | tf_op jit(solution)/shard_map/ppermute | solution.py:49
  17.7 0.7 fusion.36
  18.4 11.9 %collective-permute-done = bf16[8,16,8192]{2,1,0:T(8,128)(2,1)S(1)} collective-permute-done((bf16[8,16,8192]{2,1,0:T(8,128)(2,1)}, bf16[8,16,8192]{2,1,0:T(8,128)(2,1)S(1)}, u32[]{:S(2)}, u32[]{:S(2)}) %collective-permute-start) | collective-permute-done | bytes 2097184 | tf_op jit(solution)/shard_map/ppermute | solution.py:46
  30.3 1.9 %collective-permute-done.1 = bf16[8,16,8192]{2,1,0:T(8,128)(2,1)} collective-permute-done((bf16[8,16,8192]{2,1,0:T(8,128)(2,1)}, bf16[8,16,8192]{2,1,0:T(8,128)(2,1)}, u32[]{:S(2)}, u32[]{:S(2)}) %collective-permute-start.1) | collective-permute-done | bytes 2097184 | tf_op jit(solution)/shard_map/ppermute | solution.py:49
  32.2 5.7 %copy_bitcast_fusion = bf16[8,16,192,128]{3,1,2,0:T(8,128)(2,1)} fusion(bf16[8,16,8192]{2,1,0:T(8,128)(2,1)} %collective-permute-done.1, bf16[8,16,8192]{2,1,0:T(8,128)(2,1)} %param.12, bf16[8,16,8192]{2,1,0:T(8,128)(2,1)S(1)} %collective-permute-done), kind=kLoop, calls=%fused_computation.1 | loop fusion | flops 18874368 | bytes 12582912 | tf_op jit(solution)/shard_map/reshape | solution.py:61
  37.8 4.0 %gather_fusion = bf16[256,16,128]{2,1,0:T(8,128)(2,1)S(1)} fusion(bf16[8,16,192,128]{3,1,2,0:T(8,128)(2,1)} %copy_bitcast_fusion, s32[256]{0:T(256)S(1)} %fusion.36), kind=kCustom, calls=%fused_computation | custom fusion | bytes 2099200 | tf_op jit(solution)/shard_map/gather | solution.py:63
  41.9 0.0 copy-start.3
  41.9 0.0 copy-start.2
  41.9 0.0 copy-start.1
  41.9 0.0 slice-start
  41.9 0.0 slice-start.1
  41.9 6.9 %fusion.48 = f32[256,16,128]{2,1,0:T(8,128)S(1)} fusion(bf16[256,16,128]{2,1,0:T(8,128)(2,1)S(1)} %gather_fusion, bf16[256,128,128]{2,1,0:T(8,128)(2,1)} %param.13), kind=kOutput, calls=%fused_computation.65 | convolution fusion | flops 134217728 | bytes 11534336 | tf_op jit(solution)/shard_map/swj,sij->swi/dot_general | solution.py:64
  48.8 0.0 copy-done.3
  48.8 1.8 %fusion.7 = f32[16,128,16]{1,2,0:T(8,128)S(1)} fusion(f32[256,16,128]{2,1,0:T(8,128)S(1)} %fusion.48, f32[256]{0:T(256)S(1)} %compare_convert_fusion, s32[256]{0:T(256)S(1)} %copy-done.3), kind=kOutput, calls=%fused_computation.14 | convolution fusion | flops 100671488 | bytes 2230272 | tf_op jit(solution)/shard_map/rs,swi->wri/dot_general | solution.py:69
  50.6 0.0 copy-done.2
  50.6 0.1 bitcast_subtract_fusion
  50.7 0.0 slice-start.2
  50.7 0.0 collective-permute-done.2
  50.7 0.0 collective-permute-done.3
  50.7 0.0 copy-done.1
  50.7 6.3 %fusion.4 = bf16[16,2048]{1,0:T(8,128)(2,1)S(1)} fusion(f32[16,2048]{1,0:T(8,128)S(1)} %bitcast_subtract_fusion, bf16[2048,2304]{1,0:T(8,128)(2,1)} %param.11, bf16[16,128]{1,0:T(8,128)(2,1)S(1)} %collective-permute-done.3, bf16[16,2048]{1,0:T(8,128)(2,1)S(1)} %dynamic-slice_bitcast_fusion, bf16[16,128]{1,0:T(8,128)(2,1)S(1)} %collective-permute-done.2, ...), kind=kOutput, calls=%fused_computation.11 | convolution fusion | flops 151314432 | bytes 9715712 | tf_op jit(solution)/shard_map/dot_general | solution.py:75
  57.0 2.0 %collective-permute-start.4 = (bf16[16,128]{1,0:T(8,128)(2,1)S(1)}, bf16[16,128]{1,0:T(8,128)(2,1)S(1)}, u32[]{:S(2)}, u32[]{:S(2)}) collective-permute-start(bf16[16,128]{1,0:T(8,128)(2,1)S(1)} %get-tuple-element.8), channel_id=1, source_target_pairs={{0,4},{4,8},{8,12},{12,16},{16,20},{20,24},{24,28},{28,32},{32,36}... | collective-permute-start | bytes 12296 | tf_op jit(solution)/shard_map/ppermute | solution.py:46
  59.0 5.9 %collective-permute-start.5 = (bf16[16,128]{1,0:T(8,128)(2,1)S(1)}, bf16[16,128]{1,0:T(8,128)(2,1)S(1)}, u32[]{:S(2)}, u32[]{:S(2)}) collective-permute-start(bf16[16,128]{1,0:T(8,128)(2,1)S(1)} %get-tuple-element.9), channel_id=1, source_target_pairs={{4,0},{8,4},{12,8},{16,12},{20,16},{24,20},{28,24},{32,28},{36,32}... | collective-permute-start | bytes 12296 | tf_op jit(solution)/shard_map/ppermute | solution.py:49
  64.9 0.0 collective-permute-done.4
  64.9 1.3 %collective-permute-done.5 = bf16[16,128]{1,0:T(8,128)(2,1)S(1)} collective-permute-done((bf16[16,128]{1,0:T(8,128)(2,1)S(1)}, bf16[16,128]{1,0:T(8,128)(2,1)S(1)}, u32[]{:S(2)}, u32[]{:S(2)}) %collective-permute-start.5) | collective-permute-done | bytes 4128 | tf_op jit(solution)/shard_map/ppermute | solution.py:49
  66.2 0.0 slice-done
  66.2 0.0 slice-done.1
  66.2 0.0 slice-done.2
  66.2 2.5 %fusion.5 = bf16[16,2048]{1,0:T(8,128)(2,1)S(1)} fusion(f32[16,2048]{1,0:T(8,128)S(1)} %bitcast_subtract_fusion, bf16[2048,2304]{1,0:T(8,128)(2,1)S(1)} %bitcast.23, bf16[16,128]{1,0:T(8,128)(2,1)S(1)} %collective-permute-done.5, bf16[16,2048]{1,0:T(8,128)(2,1)S(1)} %fusion.4, bf16[16,128]{1,0:T(8,128)(2,1)S(1)} %collective-permute-done.4, ...), kind=kOutput, calls=%fused_computation.12 | convolution fusion | flops 151314432 | bytes 9715712 | tf_op jit(solution)/shard_map/dot_general | solution.py:75
  68.7 1.9 %collective-permute-start.6 = (bf16[16,128]{1,0:T(8,128)(2,1)S(1)}, bf16[16,128]{1,0:T(8,128)(2,1)S(1)}, u32[]{:S(2)}, u32[]{:S(2)}) collective-permute-start(bf16[16,128]{1,0:T(8,128)(2,1)S(1)} %get-tuple-element.6), channel_id=1, source_target_pairs={{0,4},{4,8},{8,12},{12,16},{16,20},{20,24},{24,28},{28,32},{32,36}... | collective-permute-start | bytes 12296 | tf_op jit(solution)/shard_map/ppermute | solution.py:46
  70.7 5.8 %collective-permute-start.7 = (bf16[16,128]{1,0:T(8,128)(2,1)S(1)}, bf16[16,128]{1,0:T(8,128)(2,1)S(1)}, u32[]{:S(2)}, u32[]{:S(2)}) collective-permute-start(bf16[16,128]{1,0:T(8,128)(2,1)S(1)} %get-tuple-element.7), channel_id=1, source_target_pairs={{4,0},{8,4},{12,8},{16,12},{20,16},{24,20},{28,24},{32,28},{36,32}... | collective-permute-start | bytes 12296 | tf_op jit(solution)/shard_map/ppermute | solution.py:49
  76.4 0.0 collective-permute-done.6
  76.4 1.3 %collective-permute-done.7 = bf16[16,128]{1,0:T(8,128)(2,1)S(1)} collective-permute-done((bf16[16,128]{1,0:T(8,128)(2,1)S(1)}, bf16[16,128]{1,0:T(8,128)(2,1)S(1)}, u32[]{:S(2)}, u32[]{:S(2)}) %collective-permute-start.7) | collective-permute-done | bytes 4128 | tf_op jit(solution)/shard_map/ppermute | solution.py:49
  77.7 2.5 %fusion.6 = bf16[16,2048]{1,0:T(8,128)(2,1)S(1)} fusion(f32[16,2048]{1,0:T(8,128)S(1)} %bitcast_subtract_fusion, bf16[2048,2304]{1,0:T(8,128)(2,1)S(1)} %bitcast.23, bf16[16,128]{1,0:T(8,128)(2,1)S(1)} %collective-permute-done.7, bf16[16,2048]{1,0:T(8,128)(2,1)S(1)} %fusion.5, bf16[16,128]{1,0:T(8,128)(2,1)S(1)} %collective-permute-done.6, ...), kind=kOutput, calls=%fused_computation.13 | convolution fusion | flops 151314432 | bytes 9715712 | tf_op jit(solution)/shard_map/dot_general | solution.py:75
  80.3 1.9 %collective-permute-start.8 = (bf16[16,128]{1,0:T(8,128)(2,1)S(1)}, bf16[16,128]{1,0:T(8,128)(2,1)S(1)}, u32[]{:S(2)}, u32[]{:S(2)}) collective-permute-start(bf16[16,128]{1,0:T(8,128)(2,1)S(1)} %get-tuple-element.4), channel_id=1, source_target_pairs={{0,4},{4,8},{8,12},{12,16},{16,20},{20,24},{24,28},{28,32},{32,36}... | collective-permute-start | bytes 12296 | tf_op jit(solution)/shard_map/ppermute | solution.py:46
  82.2 5.8 %collective-permute-start.9 = (bf16[16,128]{1,0:T(8,128)(2,1)S(1)}, bf16[16,128]{1,0:T(8,128)(2,1)S(1)}, u32[]{:S(2)}, u32[]{:S(2)}) collective-permute-start(bf16[16,128]{1,0:T(8,128)(2,1)S(1)} %get-tuple-element.5), channel_id=1, source_target_pairs={{4,0},{8,4},{12,8},{16,12},{20,16},{24,20},{28,24},{32,28},{36,32}... | collective-permute-start | bytes 12296 | tf_op jit(solution)/shard_map/ppermute | solution.py:49
  88.0 0.0 collective-permute-done.8
  88.0 1.3 %collective-permute-done.9 = bf16[16,128]{1,0:T(8,128)(2,1)S(1)} collective-permute-done((bf16[16,128]{1,0:T(8,128)(2,1)S(1)}, bf16[16,128]{1,0:T(8,128)(2,1)S(1)}, u32[]{:S(2)}, u32[]{:S(2)}) %collective-permute-start.9) | collective-permute-done | bytes 4128 | tf_op jit(solution)/shard_map/ppermute | solution.py:49
  89.3 3.2 %constant_dynamic-update-slice_fusion.3 = (bf16[16,8192]{1,0:T(8,128)(2,1)S(1)}, bf16[16,2048]{1,0:T(8,128)(2,1)S(1)}, f32[16,2048]{1,0:T(8,128)}) fusion(bf16[16,8192]{1,0:T(8,128)(2,1)S(1)} %broadcast_in_dim.8, s32[]{:T(128)S(6)} %select_n.36, f32[2048]{0:T(1024)S(1)} %copy-done.1, f32[16,2048]{1,0:T(8,128)S(1)} %bitcast_subtract_fusion, ...), kind=kOutput, calls=%fused_computation.50 | convolution fusion | flops 151314432 | bytes 9912324 | tf_op jit(solution)/shard_map/dot_general | solution.py:75
  92.5 1.6 %collective-permute-start.10 = (bf16[16,2048]{1,0:T(8,128)(2,1)S(1)}, bf16[16,2048]{1,0:T(8,128)(2,1)S(1)}, u32[]{:S(2)}, u32[]{:S(2)}) collective-permute-start(bf16[16,2048]{1,0:T(8,128)(2,1)S(1)} %get-tuple-element.3), channel_id=1, source_target_pairs={{0,1},{1,2},{2,3},{3,0},{4,5},{5,6},{6,7},{7,4},{8,9},{9,10},{10,1... | collective-permute-start | bytes 196616 | tf_op jit(solution)/shard_map/ppermute | solution.py:26
  94.1 1.7 %collective-permute-start.11 = (bf16[16,2048]{1,0:T(8,128)(2,1)S(1)}, bf16[16,2048]{1,0:T(8,128)(2,1)S(1)}, u32[]{:S(2)}, u32[]{:S(2)}) collective-permute-start(bf16[16,2048]{1,0:T(8,128)(2,1)S(1)} %get-tuple-element.3), channel_id=1, source_target_pairs={{0,3},{1,0},{2,1},{3,2},{4,7},{5,4},{6,5},{7,6},{8,11},{9,8},{10,9... | collective-permute-start | bytes 196616 | tf_op jit(solution)/shard_map/ppermute | solution.py:34
  95.8 2.5 %collective-permute-done.10 = bf16[16,2048]{1,0:T(8,128)(2,1)S(1)} collective-permute-done((bf16[16,2048]{1,0:T(8,128)(2,1)S(1)}, bf16[16,2048]{1,0:T(8,128)(2,1)S(1)}, u32[]{:S(2)}, u32[]{:S(2)}) %collective-permute-start.10) | collective-permute-done | bytes 65568 | tf_op jit(solution)/shard_map/ppermute | solution.py:26
  98.3 0.1 collective-permute-start.12
  98.4 0.0 collective-permute-done.11
  98.4 5.3 %collective-permute-done.12 = bf16[16,2048]{1,0:T(8,128)(2,1)S(1)} collective-permute-done((bf16[16,2048]{1,0:T(8,128)(2,1)S(1)}, bf16[16,2048]{1,0:T(8,128)(2,1)S(1)}, u32[]{:S(2)}, u32[]{:S(2)}) %collective-permute-start.12) | collective-permute-done | bytes 65568 | tf_op jit(solution)/shard_map/ppermute | solution.py:26
  103.8 0.0 copy-start
  103.8 0.7 copy-done
  (11 shorter events, 0.1 us)
Async XLA Ops:
  0.6 29.7 %collective-permute-start = (bf16[8,16,8192]{2,1,0:T(8,128)(2,1)}, bf16[8,16,8192]{2,1,0:T(8,128)(2,1)S(1)}, u32[]{:S(2)}, u32[]{:S(2)}) collective-permute-start(bf16[8,16,8192]{2,1,0:T(8,128)(2,1)} %param.12), channel_id=1, source_target_pairs={{0,4},{4,8},{8,12},{12,16},{16,20},{20,24},{24,28},{28,32},{32,36}... | collective-permute-start | bytes 6291464 | tf_op jit(solution)/shard_map/ppermute | solution.py:46
  2.6 29.6 %collective-permute-start.1 = (bf16[8,16,8192]{2,1,0:T(8,128)(2,1)}, bf16[8,16,8192]{2,1,0:T(8,128)(2,1)}, u32[]{:S(2)}, u32[]{:S(2)}) collective-permute-start(bf16[8,16,8192]{2,1,0:T(8,128)(2,1)} %param.12), channel_id=1, source_target_pairs={{4,0},{8,4},{12,8},{16,12},{20,16},{24,20},{28,24},{32,28},{36,32}... | collective-permute-start | bytes 6291464 | tf_op jit(solution)/shard_map/ppermute | solution.py:49
  9.3 41.3 %collective-permute-start.2 = (bf16[16,128]{1,0:T(8,128)(2,1)S(1)}, bf16[16,128]{1,0:T(8,128)(2,1)S(1)}, u32[]{:S(2)}, u32[]{:S(2)}) collective-permute-start(bf16[16,128]{1,0:T(8,128)(2,1)S(1)} %get-tuple-element.10), channel_id=1, source_target_pairs={{0,4},{4,8},{8,12},{12,16},{16,20},{20,24},{24,28},{28,32},{32,36}... | collective-permute-start | bytes 12296 | tf_op jit(solution)/shard_map/ppermute | solution.py:46
  11.3 39.4 %collective-permute-start.3 = (bf16[16,128]{1,0:T(8,128)(2,1)S(1)}, bf16[16,128]{1,0:T(8,128)(2,1)S(1)}, u32[]{:S(2)}, u32[]{:S(2)}) collective-permute-start(bf16[16,128]{1,0:T(8,128)(2,1)S(1)} %get-tuple-element.11), channel_id=1, source_target_pairs={{4,0},{8,4},{12,8},{16,12},{20,16},{24,20},{28,24},{32,28},{36,32}... | collective-permute-start | bytes 12296 | tf_op jit(solution)/shard_map/ppermute | solution.py:49
  41.9 7.0 %copy-start.3 = (s32[256]{0:T(256)S(1)}, s32[256]{0:T(256)}, u32[]{:S(2)}) copy-start(s32[256]{0:T(256)} %param.14) | copy-start | bytes 3076
  41.9 8.7 %copy-start.2 = (f32[16,2048]{1,0:T(8,128)S(1)}, f32[16,2048]{1,0:T(8,128)}, u32[]{:S(2)}) copy-start(f32[16,2048]{1,0:T(8,128)} %param.9) | copy-start | bytes 393220
  41.9 8.8 %copy-start.1 = (f32[2048]{0:T(1024)S(1)}, f32[2048]{0:T(1024)}, u32[]{:S(2)}) copy-start(f32[2048]{0:T(1024)} %param.10) | copy-start | bytes 24580
  41.9 24.3 %slice-start = ((s8[9437184]{0:T(1024)(128)(4,1)}), s8[4194304]{0:T(1024)(128)(4,1)S(1)}, s32[]{:S(2)}) async-start(s8[9437184]{0:T(1024)(128)(4,1)} %bitcast.22), calls=%async_computation | async-start | bytes 8388608
  41.9 24.3 %slice-start.1 = ((s8[9437184]{0:T(1024)(128)(4,1)}), s8[4194304]{0:T(1024)(128)(4,1)S(1)}, s32[]{:S(2)}) async-start(s8[9437184]{0:T(1024)(128)(4,1)} %bitcast.22), calls=%async_computation.1 | async-start | bytes 8388608
  50.7 15.5 %slice-start.2 = ((s8[9437184]{0:T(1024)(128)(4,1)}), s8[1048576]{0:T(1024)(128)(4,1)S(1)}, s32[]{:S(2)}) async-start(s8[9437184]{0:T(1024)(128)(4,1)} %bitcast.22), calls=%async_computation.2 | async-start | bytes 2097152
  57.0 7.9 %collective-permute-start.4 = (bf16[16,128]{1,0:T(8,128)(2,1)S(1)}, bf16[16,128]{1,0:T(8,128)(2,1)S(1)}, u32[]{:S(2)}, u32[]{:S(2)}) collective-permute-start(bf16[16,128]{1,0:T(8,128)(2,1)S(1)} %get-tuple-element.8), channel_id=1, source_target_pairs={{0,4},{4,8},{8,12},{12,16},{16,20},{20,24},{24,28},{28,32},{32,36}... | collective-permute-start | bytes 12296 | tf_op jit(solution)/shard_map/ppermute | solution.py:46
  59.0 7.2 %collective-permute-start.5 = (bf16[16,128]{1,0:T(8,128)(2,1)S(1)}, bf16[16,128]{1,0:T(8,128)(2,1)S(1)}, u32[]{:S(2)}, u32[]{:S(2)}) collective-permute-start(bf16[16,128]{1,0:T(8,128)(2,1)S(1)} %get-tuple-element.9), channel_id=1, source_target_pairs={{4,0},{8,4},{12,8},{16,12},{20,16},{24,20},{28,24},{32,28},{36,32}... | collective-permute-start | bytes 12296 | tf_op jit(solution)/shard_map/ppermute | solution.py:49
  68.7 7.7 %collective-permute-start.6 = (bf16[16,128]{1,0:T(8,128)(2,1)S(1)}, bf16[16,128]{1,0:T(8,128)(2,1)S(1)}, u32[]{:S(2)}, u32[]{:S(2)}) collective-permute-start(bf16[16,128]{1,0:T(8,128)(2,1)S(1)} %get-tuple-element.6), channel_id=1, source_target_pairs={{0,4},{4,8},{8,12},{12,16},{16,20},{20,24},{24,28},{28,32},{32,36}... | collective-permute-start | bytes 12296 | tf_op jit(solution)/shard_map/ppermute | solution.py:46
  70.7 7.1 %collective-permute-start.7 = (bf16[16,128]{1,0:T(8,128)(2,1)S(1)}, bf16[16,128]{1,0:T(8,128)(2,1)S(1)}, u32[]{:S(2)}, u32[]{:S(2)}) collective-permute-start(bf16[16,128]{1,0:T(8,128)(2,1)S(1)} %get-tuple-element.7), channel_id=1, source_target_pairs={{4,0},{8,4},{12,8},{16,12},{20,16},{24,20},{28,24},{32,28},{36,32}... | collective-permute-start | bytes 12296 | tf_op jit(solution)/shard_map/ppermute | solution.py:49
  80.3 7.7 %collective-permute-start.8 = (bf16[16,128]{1,0:T(8,128)(2,1)S(1)}, bf16[16,128]{1,0:T(8,128)(2,1)S(1)}, u32[]{:S(2)}, u32[]{:S(2)}) collective-permute-start(bf16[16,128]{1,0:T(8,128)(2,1)S(1)} %get-tuple-element.4), channel_id=1, source_target_pairs={{0,4},{4,8},{8,12},{12,16},{16,20},{20,24},{24,28},{28,32},{32,36}... | collective-permute-start | bytes 12296 | tf_op jit(solution)/shard_map/ppermute | solution.py:46
  82.2 7.1 %collective-permute-start.9 = (bf16[16,128]{1,0:T(8,128)(2,1)S(1)}, bf16[16,128]{1,0:T(8,128)(2,1)S(1)}, u32[]{:S(2)}, u32[]{:S(2)}) collective-permute-start(bf16[16,128]{1,0:T(8,128)(2,1)S(1)} %get-tuple-element.5), channel_id=1, source_target_pairs={{4,0},{8,4},{12,8},{16,12},{20,16},{24,20},{28,24},{32,28},{36,32}... | collective-permute-start | bytes 12296 | tf_op jit(solution)/shard_map/ppermute | solution.py:49
  92.5 5.8 %collective-permute-start.10 = (bf16[16,2048]{1,0:T(8,128)(2,1)S(1)}, bf16[16,2048]{1,0:T(8,128)(2,1)S(1)}, u32[]{:S(2)}, u32[]{:S(2)}) collective-permute-start(bf16[16,2048]{1,0:T(8,128)(2,1)S(1)} %get-tuple-element.3), channel_id=1, source_target_pairs={{0,1},{1,2},{2,3},{3,0},{4,5},{5,6},{6,7},{7,4},{8,9},{9,10},{10,1... | collective-permute-start | bytes 196616 | tf_op jit(solution)/shard_map/ppermute | solution.py:26
  94.1 4.3 %collective-permute-start.11 = (bf16[16,2048]{1,0:T(8,128)(2,1)S(1)}, bf16[16,2048]{1,0:T(8,128)(2,1)S(1)}, u32[]{:S(2)}, u32[]{:S(2)}) collective-permute-start(bf16[16,2048]{1,0:T(8,128)(2,1)S(1)} %get-tuple-element.3), channel_id=1, source_target_pairs={{0,3},{1,0},{2,1},{3,2},{4,7},{5,4},{6,5},{7,6},{8,11},{9,8},{10,9... | collective-permute-start | bytes 196616 | tf_op jit(solution)/shard_map/ppermute | solution.py:34
  98.3 5.5 %collective-permute-start.12 = (bf16[16,2048]{1,0:T(8,128)(2,1)S(1)}, bf16[16,2048]{1,0:T(8,128)(2,1)S(1)}, u32[]{:S(2)}, u32[]{:S(2)}) collective-permute-start(bf16[16,2048]{1,0:T(8,128)(2,1)S(1)} %collective-permute-done.10), channel_id=1, source_target_pairs={{0,1},{1,2},{2,3},{3,0},{4,5},{5,6},{6,7},{7,4},{8,9},{9,10},{10,1... | collective-permute-start | bytes 196616 | tf_op jit(solution)/shard_map/ppermute | solution.py:26
  103.8 0.7 copy-start
